TPU v7x, 32 devices: a whole 2x2x4 slice. The times are simulated.
32 devices in a mesh: pipe: 4 (over y, x), seq: 8 (over z, core).
Axes of the slice: x: 2, y: 2, z: 4, core: 2. Of those that a mesh axis runs over, the one named last changes fastest.
Arguments:
- in_flight: bfloat16 [4, 8192, 1024], P('pipe', 'seq'), may hold values from -6 to 6
- fresh_rows: bfloat16 [8192, 1024], P('seq'), may hold values from -6 to 6
- right_factor: bfloat16 [4, 32, 256, 256], P('pipe', 'seq'), may hold values from -0.375 to 0.375
- left_factor: bfloat16 [4, 256, 32, 32], P('pipe', 'seq'), may hold values from -1 to 1
- gate_gain: float32 [4, 1024], P('pipe'), may hold values from -4 to 4
- gate_bias: float32 [4, 1024], P('pipe'), may hold values from -4 to 4
- norm_gain: float32 [4, 1024], P('pipe'), may hold values from 0.5 to 1.5
- w_up: bfloat16 [4, 4, 256, 512], P('pipe'), may hold values from -0.375 to 0.375
- w_down: bfloat16 [4, 4, 4, 128, 256], P('pipe'), may hold values from -0.25 to 0.25
Outputs:
- first_tick: bfloat16 [4, 8192, 1024], P('pipe', 'seq')
- second_tick: bfloat16 [4, 8192, 1024], P('pipe', 'seq')
All inputs are finite; a program needn't handle non-finite values.
Results may differ from a plain program's by a relative error of at most 0.007.
Values may be sent and summed in bfloat16 or wider, within the bound.
A program may use at most 128 MiB of HBM per device.

v0:
```python
import jax
import jax.numpy as jnp
from jax import lax
from jax.sharding import PartitionSpec as P

BLOCK = 256


def shifted(block, axis, distance):
    devices = range(lax.axis_size(axis))
    route = [(i - distance, i) for i in devices if i - distance in devices]
    return lax.ppermute(block, axis, route)


def channel_part(rows, returned, gate_slope, gate_shift, gain, up_weight, down_weight):
    input_wide = rows.astype(jnp.float32)
    mixed_seq = returned.reshape(rows.shape).astype(jnp.float32)
    residual = input_wide + mixed_seq * jax.nn.sigmoid(input_wide * gate_slope + gate_shift)
    scale_row = lax.rsqrt(jnp.mean(residual * residual, axis=-1, keepdims=True) + 1e-06)
    normed = (residual * scale_row * gain).astype(jnp.bfloat16)
    blocks_count = up_weight.shape[0]
    up_proj = jnp.einsum(
        "tbd,bdf->tbf",
        normed.reshape(rows.shape[0], blocks_count, -1),
        up_weight,
        preferred_element_type=jnp.float32,
    )
    hidden = jax.nn.gelu(up_proj, approximate=True).astype(jnp.bfloat16)
    hidden = hidden.reshape(rows.shape[0], blocks_count, blocks_count, down_weight.shape[2])
    down_proj = jnp.einsum(
        "tbkq,kbqe->tke", hidden, down_weight, preferred_element_type=jnp.float32
    )
    return (residual + down_proj.reshape(rows.shape)).astype(jnp.bfloat16)


def one_layer(
    rows, right_blocks, left_blocks, gate_slope, gate_shift, gain, up_weight, down_weight
):
    tok_rows, width = rows.shape
    blocks_here = right_blocks.shape[0]
    seq_devices = lax.axis_size("seq")
    cols_here = left_blocks.shape[0]
    blocked = rows.reshape(blocks_here, BLOCK, width)
    first_mix = jnp.einsum(
        "ikj,ijc->ikc", right_blocks, blocked, preferred_element_type=jnp.float32
    ).astype(jnp.bfloat16)
    grouped = first_mix.reshape(blocks_here, seq_devices, cols_here, width)
    arrived = lax.all_to_all(grouped, "seq", split_axis=1, concat_axis=0, tiled=True)
    second_mix = jnp.einsum(
        "jpi,ijc->pjc", left_blocks, arrived[:, 0], preferred_element_type=jnp.float32
    ).astype(jnp.bfloat16)
    regrouped = second_mix.reshape(seq_devices, blocks_here, cols_here, width)
    returned = lax.all_to_all(regrouped, "seq", split_axis=0, concat_axis=2, tiled=True)
    return channel_part(rows, returned, gate_slope, gate_shift, gain, up_weight, down_weight)


def shards(
    in_flight, fresh_rows, right_factor, left_factor, gate_gain, gate_bias, norm_gain, w_up, w_down
):
    segment_index = lax.axis_index("pipe")
    weights = (
        right_factor[0],
        left_factor[0],
        gate_gain[0],
        gate_bias[0],
        norm_gain[0],
        w_up[0],
        w_down[0],
    )
    first_out = one_layer(in_flight[0], *weights)
    received = shifted(first_out, "pipe", 1)
    current = jnp.where(segment_index == 0, fresh_rows, received)
    second_out = one_layer(current, *weights)
    return (first_out[None], second_out[None])


def solution(mesh):
    in_specs = (
        P("pipe", "seq", None),
        P("seq", None),
        P("pipe", "seq", None, None),
        P("pipe", "seq", None, None),
        P("pipe", None),
        P("pipe", None),
        P("pipe", None),
        P("pipe", None, None, None),
        P("pipe", None, None, None, None),
    )
    out_specs = (P("pipe", "seq", None), P("pipe", "seq", None))
    return jax.shard_map(shards, mesh=mesh, in_specs=in_specs, out_specs=out_specs, check_vma=False)
```

profile of v0, /device:TPU:9, one launch (start us, length us, event | category | flops | bytes accessed | tf_op | source)
XLA Modules:
  0.0 345.2 jit_solution(17335495609176930946)
XLA Ops:
  3.5 51.4 %all_to_all.48 = bf16[4,8,32,1024]{3,2,0,1:T(8,128)(2,1)S(1)} all-to-all(bf16[4,8,32,1024]{3,2,0,1:T(8,128)(2,1)S(1)} %copy.61), channel_id=1, replica_groups=mesh['pipe'=4,'seq'=8] {'seq'}, dimensions={1} | all-to-all | bytes 4194304 | tf_op jit(solution)/shard_map/all_to_all | solution.py:48
  60.4 7.4 %all-to-all-start.1 = ((bf16[8,4,32,1024]{3,2,1,0:T(8,128)(2,1)}), bf16[8,4,32,1024]{3,2,1,0:T(8,128)(2,1)}, u32[]{:S(2)}, u32[]{:S(2)}) async-start(bf16[8,4,32,1024]{3,2,1,0:T(8,128)(2,1)} %bitcast.135), calls=%async_computation.1 | async-start | bytes 4194304 | tf_op jit(solution)/shard_map/all_to_all | solution.py:53
  67.8 3.4 reshape.136
  73.8 39.5 %all-to-all-done.1 = bf16[8,4,32,1024]{3,2,1,0:T(8,128)(2,1)} async-done(((bf16[8,4,32,1024]{3,2,1,0:T(8,128)(2,1)}), bf16[8,4,32,1024]{3,2,1,0:T(8,128)(2,1)}, u32[]{:S(2)}, u32[]{:S(2)}) %all-to-all-start.1) | async-done | bytes 2097184 | tf_op jit(solution)/shard_map/all_to_all | solution.py:53
  113.2 6.0 %bitcast_convert_fusion.1 = (f32[8,1,4,32,1024]{4,3,0,2,1:T(8,128)}, f32[1,4,8,32,1024]{4,3,2,1,0:T(8,128)}) fusion(bf16[8,4,32,1024]{3,2,1,0:T(8,128)(2,1)} %all-to-all-done.1), kind=kLoop, calls=%fused_computation.52 | loop fusion | flops 1048576 | bytes 10485760 | tf_op jit(solution)/shard_map/convert_element_type | solution.py:17
  119.2 5.6 %reshape.137 = f32[1024,4,256]{2,1,0:T(4,128)} reshape(f32[1,4,8,32,1024]{4,3,2,1,0:T(8,128)} %get-tuple-element.5) | data formatting | bytes 8388608 | tf_op jit(solution)/shard_map/convert_element_type | solution.py:17
  124.8 3.9 %multiply_reduce_fusion.1 = f32[1024]{0:T(1024)S(1)} fusion(f32[1024]{0:T(1024)S(1)} %bitcast.143, f32[1024]{0:T(1024)S(1)} %bitcast.147, f32[8,1,4,32,1024]{4,3,0,2,1:T(8,128)} %get-tuple-element.4, bf16[1,1024,1024]{2,1,0:T(8,128)(2,1)S(1)} %copy-done.1), kind=kLoop, calls=%fused_computation.45 | loop fusion | flops 10484736 | bytes 6303744 | tf_op jit(solution)/shard_map/reduce_sum | solution.py:19
  128.8 5.4 %multiply_convert_fusion.1 = bf16[1024,4,256]{2,1,0:T(4,128)(2,1)S(1)} fusion(f32[1024,4,256]{2,1,0:T(4,128)S(1)} %copy-done.5, f32[1024,4,256]{2,1,0:T(4,128)} %reshape.137, f32[4,256]{1,0:T(4,128)S(1)} %mul.122, f32[1024]{0:T(1024)S(1)} %add_rsqrt_fusion.1, f32[4,256]{1,0:T(4,128)S(1)} %add.94, f32[4,256]{1,0:T(4,128)S(1)} %mul.112), kind=kLoop, calls=%fused_computation.44 | loop fusion | flops 10485760 | bytes 10502144 | tf_op jit(solution)/shard_map/convert_element_type | solution.py:20
  134.2 3.3 fusion.7
  137.5 3.3 fusion.48
  140.8 5.4 %copy.70 = f32[1024,1024]{1,0:T(8,128)} copy(f32[1024,1024]{0,1:T(8,128)} %bitcast.131) | data formatting | bytes 8388608 | tf_op jit(solution)/shard_map/reshape | solution.py:33
  146.2 6.3 %add_convert_fusion.1 = bf16[1024,1024]{1,0:T(8,128)(2,1)} fusion(f32[1024,1024]{1,0:T(8,128)} %copy.70, f32[1024]{0:T(1024)S(1)} %bitcast.144, f32[1024]{0:T(1024)S(1)} %bitcast.148, f32[8,1,4,32,1024]{4,3,0,2,1:T(8,128)} %get-tuple-element.4, bf16[1,1024,1024]{2,1,0:T(8,128)(2,1)S(1)} %copy-done.1), kind=kLoop, calls=%fused_computation.43 | loop fusion | flops 10485760 | bytes 12591104 | tf_op jit(solution)/shard_map/convert_element_type | solution.py:33
  152.5 4.5 %collective-permute-start = (bf16[1024,1024]{1,0:T(8,128)(2,1)}, bf16[1024,1024]{1,0:T(8,128)(2,1)}, u32[]{:S(2)}, u32[]{:S(2)}) collective-permute-start(bf16[1024,1024]{1,0:T(8,128)(2,1)} %add_convert_fusion.1), channel_id=1, source_target_pairs={{0,8},{8,16},{16,24},{1,9},{9,17},{17,25},{2,10},{10,18},{18,26},{... | collective-permute-start | bytes 6291464 | tf_op jit(solution)/shard_map/ppermute | solution.py:12
  157.0 43.5 %collective-permute-done = bf16[1024,1024]{1,0:T(8,128)(2,1)} collective-permute-done((bf16[1024,1024]{1,0:T(8,128)(2,1)}, bf16[1024,1024]{1,0:T(8,128)(2,1)}, u32[]{:S(2)}, u32[]{:S(2)}) %collective-permute-start) | collective-permute-done | bytes 2097184 | tf_op jit(solution)/shard_map/ppermute | solution.py:12
  203.6 52.8 %all_to_all.49 = bf16[4,8,32,1024]{3,2,0,1:T(8,128)(2,1)S(1)} all-to-all(bf16[4,8,32,1024]{3,2,0,1:T(8,128)(2,1)S(1)} %copy.71), channel_id=1, replica_groups=mesh['pipe'=4,'seq'=8] {'seq'}, dimensions={1} | all-to-all | bytes 4194304 | tf_op jit(solution)/shard_map/all_to_all | solution.py:48
  256.4 4.3 %convert_bitcast_fusion = bf16[32,32,1024]{2,0,1:T(8,128)(2,1)} fusion(bf16[32,32,1024]{2,1,0:T(8,128)(2,1)S(1)} %bitcast.137, bf16[1,32,32,32]{3,2,1,0:T(8,128)(2,1)S(1)} %copy-done.9), kind=kOutput, calls=%fused_computation.56 | convolution fusion | flops 68157440 | bytes 4259840 | tf_op jit(solution)/shard_map/jpi,ijc->pjc/dot_general | solution.py:49
  260.7 4.1 %reshape.131 = bf16[8,4,32,1024]{3,1,0,2:T(4,128)(2,1)} reshape(bf16[32,32,1024]{2,0,1:T(8,128)(2,1)} %convert_bitcast_fusion) | data formatting | bytes 4194304 | tf_op jit(solution)/shard_map/reshape | solution.py:52
  264.8 3.8 %copy.73 = bf16[8,4,32,1024]{3,1,2,0:T(4,128)(2,1)} copy(bf16[8,4,32,1024]{3,1,0,2:T(4,128)(2,1)} %reshape.131) | data formatting | bytes 4194304 | tf_op jit(solution)/shard_map/reshape | solution.py:52
  268.6 7.4 %all-to-all-start.3 = ((bf16[8,4,32,1024]{3,1,2,0:T(4,128)(2,1)}), bf16[8,4,32,1024]{3,1,2,0:T(4,128)(2,1)}, u32[]{:S(2)}, u32[]{:S(2)}) async-start(bf16[8,4,32,1024]{3,1,2,0:T(4,128)(2,1)} %copy.73), calls=%async_computation.3 | async-start | bytes 4194304 | tf_op jit(solution)/shard_map/all_to_all | solution.py:53
  276.0 5.4 %copy.69 = f32[1,1024,1024]{2,1,0:T(8,128)} copy(f32[1,1024,1024]{1,2,0:T(8,128)} %bitcast.132) | data formatting | bytes 8388608 | tf_op jit(solution)/shard_map/reshape | solution.py:33
  281.3 6.3 %fusion.26 = bf16[1,1024,1024]{2,1,0:T(8,128)(2,1)} fusion(f32[1,1024,1024]{2,1,0:T(8,128)} %copy.69, f32[8,1,4,32,1024]{4,3,0,2,1:T(8,128)} %get-tuple-element.4, f32[1024]{0:T(1024)S(1)} %bitcast.145, f32[1024]{0:T(1024)S(1)} %bitcast.149, bf16[1,1024,1024]{2,1,0:T(8,128)(2,1)S(1)} %copy-done.1), kind=kLoop, calls=%fused_computation.33 | loop fusion | flops 10485760 | bytes 12591104 | tf_op jit(solution)/shard_map/convert_element_type | solution.py:33
  287.7 33.8 %all-to-all-done.3 = bf16[8,4,32,1024]{3,1,2,0:T(4,128)(2,1)} async-done(((bf16[8,4,32,1024]{3,1,2,0:T(4,128)(2,1)}), bf16[8,4,32,1024]{3,1,2,0:T(4,128)(2,1)}, u32[]{:S(2)}, u32[]{:S(2)}) %all-to-all-start.3) | async-done | bytes 2097184 | tf_op jit(solution)/shard_map/all_to_all | solution.py:53
  334.3 5.4 %copy.79 = f32[1024,1024]{1,0:T(8,128)} copy(f32[1024,1024]{0,1:T(8,128)} %bitcast.134) | data formatting | bytes 8388608 | tf_op jit(solution)/shard_map/reshape | solution.py:33
  339.7 5.5 %fusion.32 = bf16[1,1024,1024]{2,1,0:T(8,128)(2,1)} fusion(f32[1024,1024]{1,0:T(8,128)} %copy-done.2, f32[1024,1024]{1,0:T(8,128)} %copy.79), kind=kLoop, calls=%fused_computation.46 | loop fusion | flops 2097152 | bytes 10485760 | tf_op jit(solution)/shard_map/broadcast_in_dim | solution.py:74
  (47 shorter events, 26.8 us)
Async XLA Ops:
  0.6 133.6 %copy-start = (bf16[1,4,256,512]{3,2,1,0:T(8,128)(2,1)S(1)}, bf16[1,4,256,512]{3,2,1,0:T(8,128)(2,1)}, u32[]{:S(2)}) copy-start(bf16[1,4,256,512]{3,2,1,0:T(8,128)(2,1)} %param.16) | copy-start | bytes 3145732
  3.2 51.7 %copy-start.9 = (bf16[1,32,32,32]{3,2,1,0:T(8,128)(2,1)S(1)}, bf16[1,32,32,32]{3,2,1,0:T(8,128)(2,1)}, u32[]{:S(2)}) copy-start(bf16[1,32,32,32]{3,2,1,0:T(8,128)(2,1)} %param.12) | copy-start | bytes 196612
  57.9 9.9 %copy-start.1 = (bf16[1,1024,1024]{2,1,0:T(8,128)(2,1)S(1)}, bf16[1,1024,1024]{2,1,0:T(8,128)(2,1)}, u32[]{:S(2)}) copy-start(bf16[1,1024,1024]{2,1,0:T(8,128)(2,1)} %param.9) | copy-start | bytes 6291460
  60.4 52.9 %all-to-all-start.1 = ((bf16[8,4,32,1024]{3,2,1,0:T(8,128)(2,1)}), bf16[8,4,32,1024]{3,2,1,0:T(8,128)(2,1)}, u32[]{:S(2)}, u32[]{:S(2)}) async-start(bf16[8,4,32,1024]{3,2,1,0:T(8,128)(2,1)} %bitcast.135), calls=%async_computation.1 | async-start | bytes 4194304 | tf_op jit(solution)/shard_map/all_to_all | solution.py:53
  67.7 4.0 %copy-start.12 = (f32[1,1024]{1,0:T(1,128)S(1)}, f32[1,1024]{1,0:T(1,128)}, u32[]{:S(2)}) copy-start(f32[1,1024]{1,0:T(1,128)} %param.15) | copy-start | bytes 12292
  67.7 4.6 %copy-start.10 = (f32[1,1024]{1,0:T(1,128)S(1)}, f32[1,1024]{1,0:T(1,128)}, u32[]{:S(2)}) copy-start(f32[1,1024]{1,0:T(1,128)} %param.14) | copy-start | bytes 12292
  67.7 5.3 %copy-start.11 = (f32[1,1024]{1,0:T(1,128)S(1)}, f32[1,1024]{1,0:T(1,128)}, u32[]{:S(2)}) copy-start(f32[1,1024]{1,0:T(1,128)} %param.13) | copy-start | bytes 12292
  124.8 3.9 %copy-start.5 = (f32[1024,4,256]{2,1,0:T(4,128)S(1)}, f32[1024,4,256]{2,1,0:T(4,128)}, u32[]{:S(2)}) copy-start(f32[1024,4,256]{2,1,0:T(4,128)} %reshape.136) | copy-start | bytes 12582916
  134.2 3.3 copy-start.6
  152.5 48.0 %collective-permute-start = (bf16[1024,1024]{1,0:T(8,128)(2,1)}, bf16[1024,1024]{1,0:T(8,128)(2,1)}, u32[]{:S(2)}, u32[]{:S(2)}) collective-permute-start(bf16[1024,1024]{1,0:T(8,128)(2,1)} %add_convert_fusion.1), channel_id=1, source_target_pairs={{0,8},{8,16},{16,24},{1,9},{9,17},{17,25},{2,10},{10,18},{18,26},{... | collective-permute-start | bytes 6291464 | tf_op jit(solution)/shard_map/ppermute | solution.py:12
  157.0 45.3 %copy-start.8 = (bf16[1,4,256,256]{3,2,1,0:T(8,128)(2,1)S(1)}, bf16[1,4,256,256]{3,2,1,0:T(8,128)(2,1)}, u32[]{:S(2)}) copy-start(bf16[1,4,256,256]{3,2,1,0:T(8,128)(2,1)} %param.11) | copy-start | bytes 1572868
  202.3 1.3 copy-start.3
  268.6 52.9 %all-to-all-start.3 = ((bf16[8,4,32,1024]{3,1,2,0:T(4,128)(2,1)}), bf16[8,4,32,1024]{3,1,2,0:T(4,128)(2,1)}, u32[]{:S(2)}, u32[]{:S(2)}) async-start(bf16[8,4,32,1024]{3,1,2,0:T(4,128)(2,1)} %copy.73), calls=%async_computation.3 | async-start | bytes 4194304 | tf_op jit(solution)/shard_map/all_to_all | solution.py:53
  287.7 36.1 %copy-start.4 = (bf16[1024,1024]{1,0:T(8,128)(2,1)S(1)}, bf16[1024,1024]{1,0:T(8,128)(2,1)}, u32[]{:S(2)}) copy-start(bf16[1024,1024]{1,0:T(8,128)(2,1)} %copy-done.3) | copy-start | bytes 6291460
  325.4 1.9 copy-start.2
  327.8 3.3 copy-start.7
where the time goes:
time: 351 us; the launch traced here: 345 us
  waiting for transfers between devices  117 us (33%)
  blocking collectives  104 us (30%)
  other arithmetic  41.7 us (12%)
  local copies, waits for them, and re-layouts  38.9 us (11%)
  matrix products  23.6 us (7%)
  starting transfers between devices  19.2 us (5%)
    all_to_all x2, blocking collectives, one_layer(): lax.all_to_all(grouped, 'seq', split_axis=1, concat_axis=0, tiled=True)  104 us
    all_to_all x2, waiting for transfers between devices, one_layer(): lax.all_to_all(regrouped, 'seq', split_axis=0, concat_axis=2, tiled=True)  73.3 us
    ppermute x1, waiting for transfers between devices, shifted(): return lax.ppermute(block, axis, route)  43.5 us
    reshape x3, local copies, waits for them, and re-layouts, channel_part(): return (residual + down_proj.reshape(rows.shape)).astype(jnp.bfloat16)  16.1 us
    all_to_all x2, starting transfers between devices, one_layer(): lax.all_to_all(regrouped, 'seq', split_axis=0, concat_axis=2, tiled=True)  14.8 us
    convert_element_type x2, other arithmetic, channel_part(): return (residual + down_proj.reshape(rows.shape)).astype(jnp.bfloat16)  12.7 us
    reshape x3, local copies, waits for them, and re-layouts, one_layer(): regrouped = second_mix.reshape(seq_devices, blocks_here, cols_here, width)  10.3 us
    convert_element_type x2, other arithmetic, channel_part(): mixed_seq = returned.reshape(rows.shape).astype(jnp.float32)  8.29 us
  transfers between devices with their start and end apart: 3, of which 3 were waited for; matrix products, arithmetic and copies ran while one was open for 5% of the time, Pallas kernels for 0%

commit v1 on v0

--- a/solution.py
+++ b/solution.py
@@ -1,9 +1,16 @@
+import functools
+
 import jax
 import jax.numpy as jnp
 from jax import lax
+from jax.experimental import pallas as pl
+from jax.experimental.pallas import tpu as pltpu
 from jax.sharding import PartitionSpec as P
 
 BLOCK = 256
+GROUP = 16
+VMEM_LIMIT = 56 * 1024 * 1024
+MESH = pl.DeviceIdType.MESH
 
 
 def shifted(block, axis, distance):
@@ -74,7 +81,245 @@
     return (first_out[None], second_out[None])
 
 
+def relay_kernel(
+    sections, peers,
+    rows_ref, fresh_ref, right_ref, left_ref, slope_ref, shift_ref, gain_ref, up_ref, down_ref,
+    first_ref, second_ref,
+    mixed, arrived, spread, returned, relayed, expanded, hidden, residuals,
+    send_sem, recv_sem, relay_send, relay_recv,
+):
+    here = lax.axis_index("seq")
+    section = lax.axis_index("pipe")
+    blocks_here, block, width = rows_ref.shape
+    cols = block // peers
+    half = peers // 2
+    offsets = sorted(range(1, peers), key=lambda d: abs(d - half))
+
+    def partner(offset):
+        return lax.rem(here + offset, peers)
+
+    def own_rows(device):
+        return pl.ds(pl.multiple_of(device * cols, cols), cols)
+
+    barrier = pltpu.get_barrier_semaphore()
+    for offset in offsets:
+        pl.semaphore_signal(
+            barrier, inc=1, device_id=(section, partner(offset)), device_id_type=MESH
+        )
+
+    for other in (section + 1, section + sections - 1):
+        pl.semaphore_signal(
+            barrier, inc=1, device_id=(lax.rem(other, sections), here), device_id_type=MESH
+        )
+    pl.semaphore_wait(barrier, peers + 1)
+
+    def out_copy(tick, b, device, owner):
+        return pltpu.make_async_remote_copy(
+            src_ref=mixed.at[tick, b, own_rows(device)],
+            dst_ref=arrived.at[tick, owner * blocks_here + b],
+            send_sem=send_sem.at[tick, 0, b, device],
+            recv_sem=recv_sem.at[tick, 0, b, owner],
+            device_id=(section, device),
+            device_id_type=MESH,
+        )
+
+    def back_copy(tick, b, device, owner):
+        return pltpu.make_async_remote_copy(
+            src_ref=spread.at[tick, device * blocks_here + b],
+            dst_ref=returned.at[tick, b, own_rows(owner)],
+            send_sem=send_sem.at[tick, 1, b, device],
+            recv_sem=recv_sem.at[tick, 1, b, owner],
+            device_id=(section, device),
+            device_id_type=MESH,
+        )
+
+    def relay_copy(b):
+        return pltpu.make_async_remote_copy(
+            src_ref=first_ref.at[b],
+            dst_ref=relayed.at[b],
+            send_sem=relay_send.at[b],
+            recv_sem=relay_recv.at[b],
+            device_id=(lax.rem(section + 1, sections), here),
+            device_id_type=MESH,
+        )
+
+    def first_factor(tick, b, source):
+        mixed[tick, b] = jnp.dot(
+            right_ref[b], source[b], preferred_element_type=jnp.float32
+        ).astype(jnp.bfloat16)
+        for offset in offsets:
+            out_copy(tick, b, partner(offset), here).start()
+        arrived[tick, here * blocks_here + b] = mixed[tick, b, own_rows(here)]
+
+    def second_factor(tick):
+        def wait_block(b, carry):
+            for offset in offsets:
+                out_copy(tick, b, here, partner(offset)).wait_recv()
+            return carry
+
+        lax.fori_loop(0, blocks_here, wait_block, 0)
+        piece = width // 2
+        for g in range(cols // GROUP):
+            band = slice(g * GROUP, (g + 1) * GROUP)
+            for c in range(0, width, piece):
+                taken = arrived[tick, :, band, c : c + piece].reshape(-1, piece)
+                product = jnp.dot(expanded[g], taken, preferred_element_type=jnp.float32)
+                spread[tick, :, band, c : c + piece] = product.astype(jnp.bfloat16).reshape(
+                    -1, GROUP, piece
+                )
+
+        def send_block(b, carry):
+            for offset in offsets:
+                back_copy(tick, b, partner(offset), here).start()
+            returned[tick, b, own_rows(here)] = spread[tick, here * blocks_here + b]
+            return carry
+
+        lax.fori_loop(0, blocks_here, send_block, 0)
+
+    def channel_block(tick, b, source, target):
+        for offset in offsets:
+            back_copy(tick, b, here, partner(offset)).wait_recv()
+        wide = source[b].astype(jnp.float32)
+        gate = jax.nn.sigmoid(wide * slope_ref[...] + shift_ref[...])
+        residual = wide + returned[tick, b].astype(jnp.float32) * gate
+        residuals[...] = residual
+        scale = lax.rsqrt(jnp.mean(residual * residual, axis=-1, keepdims=True) + 1e-06)
+        parts = up_ref.shape[0]
+        step = width // parts
+        q = up_ref.shape[2] // parts
+        for p in range(parts):
+            band = slice(p * step, (p + 1) * step)
+            normed = (residuals[:, band] * scale * gain_ref[:, band]).astype(jnp.bfloat16)
+            up = jnp.dot(normed, up_ref[p], preferred_element_type=jnp.float32)
+            act = jax.nn.gelu(up, approximate=True).astype(jnp.bfloat16)
+            for k in range(parts):
+                hidden[k, :, p * q : (p + 1) * q] = act[:, k * q : (k + 1) * q]
+        for k in range(parts):
+            band = slice(k * step, (k + 1) * step)
+            down = jnp.dot(hidden[k], down_ref[k], preferred_element_type=jnp.float32)
+            target[b, :, band] = (residuals[:, band] + down).astype(jnp.bfloat16)
+
+    def opening(b, carry):
+        first_factor(0, b, rows_ref)
+        return carry
+
+    lax.fori_loop(0, blocks_here, opening, 0)
+
+    total = left_ref.shape[2]
+    size = total * GROUP
+    picks = lax.broadcasted_iota(jnp.int32, (total, size), 1) // GROUP
+    repeat = (picks == lax.broadcasted_iota(jnp.int32, (total, size), 0)).astype(jnp.bfloat16)
+    same = lax.rem(lax.broadcasted_iota(jnp.int32, (size, size), 0), GROUP) == lax.rem(
+        lax.broadcasted_iota(jnp.int32, (size, size), 1), GROUP
+    )
+    for g in range(cols // GROUP):
+        repeated = jnp.dot(left_ref[g], repeat, preferred_element_type=jnp.float32)
+        expanded[g] = jnp.where(same, repeated, 0.0).astype(jnp.bfloat16)
+
+    @pl.when(section == 0)
+    def _():
+        relayed[...] = fresh_ref[...]
+
+    second_factor(0)
+
+    def enter(b):
+        @pl.when(section > 0)
+        def _():
+            relay_copy(b).wait_recv()
+
+        first_factor(1, b, relayed)
+
+    def middle(b, carry):
+        channel_block(0, b, rows_ref, first_ref)
+
+        @pl.when(section < sections - 1)
+        def _():
+            relay_copy(b).start()
+
+        @pl.when(b > 0)
+        def _():
+            enter(b - 1)
+
+        return carry
+
+    lax.fori_loop(0, blocks_here, middle, 0)
+    enter(blocks_here - 1)
+    second_factor(1)
+
+    def closing(b, carry):
+        channel_block(1, b, relayed, second_ref)
+        return carry
+
+    lax.fori_loop(0, blocks_here, closing, 0)
+
+    def drain(b, carry):
+        for offset in offsets:
+            for tick in range(2):
+                out_copy(tick, b, partner(offset), here).wait_send()
+                back_copy(tick, b, partner(offset), here).wait_send()
+
+        @pl.when(section < sections - 1)
+        def _():
+            relay_copy(b).wait_send()
+
+        return carry
+
+    lax.fori_loop(0, blocks_here, drain, 0)
+
+
+def relay_shards(
+    in_flight, fresh_rows, right_factor, left_factor, gate_gain, gate_bias, norm_gain, w_up, w_down
+):
+    sections, peers = lax.axis_size("pipe"), lax.axis_size("seq")
+    blocks_here = right_factor.shape[1]
+    cols, total = left_factor.shape[1:3]
+    width = fresh_rows.shape[1]
+    groups = cols // GROUP
+    blocked = (blocks_here, BLOCK, width)
+    parts, step, wide = w_up.shape[1:]
+    left = left_factor[0].reshape(groups, GROUP, total, total).transpose(0, 2, 1, 3)
+    left = left.reshape(groups, total * GROUP, total)
+    whole = pl.BlockSpec(memory_space=pltpu.VMEM)
+    bf16 = jnp.bfloat16
+    first, second = pl.pallas_call(
+        functools.partial(relay_kernel, sections, peers),
+        out_shape=[jax.ShapeDtypeStruct(blocked, bf16)] * 2,
+        in_specs=[whole] * 9,
+        out_specs=[whole] * 2,
+        scratch_shapes=[
+            pltpu.VMEM((2, blocks_here, BLOCK, width), bf16),
+            pltpu.VMEM((2, total, cols, width), bf16),
+            pltpu.VMEM((2, total, cols, width), bf16),
+            pltpu.VMEM((2, blocks_here, BLOCK, width), bf16),
+            pltpu.VMEM(blocked, bf16),
+            pltpu.VMEM((groups, total * GROUP, total * GROUP), bf16),
+            pltpu.VMEM((parts, BLOCK, wide), bf16),
+            pltpu.VMEM((BLOCK, width), jnp.float32),
+            pltpu.SemaphoreType.DMA((2, 2, blocks_here, peers)),
+            pltpu.SemaphoreType.DMA((2, 2, blocks_here, peers)),
+            pltpu.SemaphoreType.DMA((blocks_here,)),
+            pltpu.SemaphoreType.DMA((blocks_here,)),
+        ],
+        compiler_params=pltpu.CompilerParams(
+            collective_id=0, has_side_effects=True, vmem_limit_bytes=VMEM_LIMIT
+        ),
+    )(
+        in_flight.reshape(blocked),
+        fresh_rows.reshape(blocked),
+        right_factor[0],
+        left,
+        gate_gain,
+        gate_bias,
+        norm_gain,
+        w_up[0],
+        w_down.reshape(parts, wide, step),
+    )
+    return first.reshape(in_flight.shape), second.reshape(in_flight.shape)
+
+
 def solution(mesh):
+    peers = mesh.shape["seq"]
+    body = relay_shards if BLOCK % (peers * GROUP) == 0 else shards
     in_specs = (
         P("pipe", "seq", None),
         P("seq", None),
@@ -87,4 +332,4 @@
         P("pipe", None, None, None, None),
     )
     out_specs = (P("pipe", "seq", None), P("pipe", "seq", None))
-    return jax.shard_map(shards, mesh=mesh, in_specs=in_specs, out_specs=out_specs, check_vma=False)
+    return jax.shard_map(body, mesh=mesh, in_specs=in_specs, out_specs=out_specs, check_vma=False)

time: 351 us -> 204 us (0.58); the launches traced: 345 us -> 204 us
  Pallas kernels: 0 us -> 197 us
  waiting for transfers between devices: 117 us -> 0 us
  blocking collectives: 104 us -> 0 us
  other arithmetic: 41.7 us -> 0 us
  local copies, waits for them, and re-layouts: 38.9 us -> 6.31 us
  matrix products: 23.6 us -> 0 us
  starting transfers between devices: 19.2 us -> 0 us
    pallas_call x0 -> x1, Pallas kernels: none -> 197 us  [relay_shards(): pl.pallas_call(functools.partial(relay_kernel, sections, peers), out_shap...]
    all_to_all x2 -> x0, blocking collectives: 104 us -> none  [one_layer(): lax.all_to_all(grouped, 'seq', split_axis=1, concat_axis=0, tiled=True)]
    all_to_all x2 -> x0, waiting for transfers between devices: 73.3 us -> none  [one_layer(): lax.all_to_all(regrouped, 'seq', split_axis=0, concat_axis=2, tiled=True)]
    ppermute x1 -> x0, waiting for transfers between devices: 43.5 us -> none  [shifted(): return lax.ppermute(block, axis, route)]
    reshape x8 -> x0, local copies, waits for them, and re-layouts: 27 us -> none  [the longest x3 16.1 us: channel_part(): return (residual + down_proj.reshape(rows.shape)).astype(jnp.bfloat16)]
    convert_element_type x6 -> x0, other arithmetic: 26.8 us -> none  [the longest x2 12.7 us: channel_part(): return (residual + down_proj.reshape(rows.shape)).astype(jnp.bfloat16)]
    dot_general x8 -> x0, matrix products: 23.6 us -> none  [the longest x2 7.32 us: one_layer(): jnp.einsum('jpi,ijc->pjc', left_blocks, arrived[:, 0], preferred_element_...]
    all_to_all x2 -> x0, starting transfers between devices: 14.8 us -> none  [one_layer(): lax.all_to_all(regrouped, 'seq', split_axis=0, concat_axis=2, tiled=True)]
  transfers between devices with their start and end apart: 3 -> 0, of which waited for: 3 -> 0; matrix products, arithmetic and copies ran while one was open for 5% -> 0% of each run, Pallas kernels for 0% -> 0%
where the time goes in v1:
time: 204 us
  Pallas kernels  197 us (97%)
  local copies, waits for them, and re-layouts  6.31 us (3%)
    pallas_call x1, Pallas kernels, relay_shards(): pl.pallas_call(functools.partial(relay_kernel, sections, peers), out_shap...  197 us
    unnamed x4, local copies, waits for them, and re-layouts  4.55 us

profile of v1, /device:TPU:9, one launch (start us, length us, event | category | flops | bytes accessed | tf_op | source)
XLA Modules:
  0.0 204.1 jit_solution(5191401035954961799)
XLA Ops:
  0.6 1.8 copy.11
  2.4 197.1 %shard_map.104 = (bf16[4,256,1024]{2,1,0:T(8,128)(2,1)}, bf16[4,256,1024]{2,1,0:T(8,128)(2,1)}) custom-call(bf16[4,256,1024]{2,1,0:T(8,128)(2,1)} %bitcast.13, bf16[4,256,1024]{2,1,0:T(8,128)(2,1)} %bitcast.14, bf16[4,256,256]{2,1,0:T(8,128)(2,1)} %bitcast.18, bf16[2,512,32]{2,1,0:T(8,128)(2,1)} %bitcast.17, f32[1,1024]{1,0:T(1,128)} %slope_ref.1, ...), custom_call_target="tpu_custom_call" | custom-call | tf_op jit(solution)/shard_map/pallas_call | solution.py:284
  199.5 0.0 copy-start
  199.5 3.2 %copy.14 = bf16[1,1024,1024]{2,1,0:T(8,128)(2,1)} copy(bf16[1,1024,1024]{2,1,0:T(8,128)(2,1)} %bitcast.12) | data formatting | bytes 4194304
  202.7 0.0 copy-done
  202.8 1.3 copy.15
Async XLA Ops:
  199.5 3.2 %copy-start = (bf16[4,256,1024]{2,1,0:T(8,128)(2,1)S(1)}, bf16[4,256,1024]{2,1,0:T(8,128)(2,1)}, u32[]{:S(2)}) copy-start(bf16[4,256,1024]{2,1,0:T(8,128)(2,1)} %get-tuple-element.5) | copy-start | bytes 6291460

commit v2 on v1

--- a/solution.py
+++ b/solution.py
@@ -83,16 +83,19 @@
 
 def relay_kernel(
     sections, peers,
-    rows_ref, fresh_ref, right_ref, left_ref, slope_ref, shift_ref, gain_ref, up_ref, down_ref,
-    first_ref, second_ref,
+    rows_hbm, fresh_hbm, right_hbm, left_hbm, slope_ref, shift_ref, gain_ref, up_hbm, down_hbm,
+    first_hbm, second_hbm,
+    rows_ref, right_ref, left_ref, up_ref, down_ref, first_ref, second_ref,
     mixed, arrived, spread, returned, relayed, expanded, hidden, residuals,
-    send_sem, recv_sem, relay_send, relay_recv,
+    send_sem, recv_sem, relay_send, relay_recv, load_sem, weight_sem, fresh_sem, store_sem,
 ):
     here = lax.axis_index("seq")
     section = lax.axis_index("pipe")
     blocks_here, block, width = rows_ref.shape
     cols = block // peers
     half = peers // 2
+    groups = cols // GROUP
+    last = blocks_here - 1
     offsets = sorted(range(1, peers), key=lambda d: abs(d - half))
 
     def partner(offset):
@@ -100,6 +103,25 @@
 
     def own_rows(device):
         return pl.ds(pl.multiple_of(device * cols, cols), cols)
+
+    def load_rows(b):
+        return pltpu.make_async_copy(rows_hbm.at[b], rows_ref.at[b], load_sem.at[0, b])
+
+    def load_right(b):
+        return pltpu.make_async_copy(right_hbm.at[b], right_ref.at[b], load_sem.at[1, b])
+
+    load_left = pltpu.make_async_copy(left_hbm, left_ref, weight_sem.at[0])
+    load_up = pltpu.make_async_copy(up_hbm, up_ref, weight_sem.at[1])
+    load_down = pltpu.make_async_copy(down_hbm, down_ref, weight_sem.at[2])
+    load_fresh = pltpu.make_async_copy(fresh_hbm, relayed, fresh_sem)
+
+    def store(tick, b):
+        source, target = ((first_ref, first_hbm), (second_ref, second_hbm))[tick]
+        return pltpu.make_async_copy(source.at[b], target.at[b], store_sem.at[tick, b])
+
+    for b in range(blocks_here):
+        load_right(b).start()
+        load_rows(b).start()
 
     barrier = pltpu.get_barrier_semaphore()
     for offset in offsets:
@@ -113,22 +135,28 @@
         )
     pl.semaphore_wait(barrier, peers + 1)
 
-    def out_copy(tick, b, device, owner):
+    def out_copy(tick, b, device, owner, piece=None):
+        start, count = (0, cols) if piece is None else (piece * GROUP, GROUP)
+        slot = b if piece is None else last + piece
+        rows = pl.ds(pl.multiple_of(device * cols + start, count), count)
         return pltpu.make_async_remote_copy(
-            src_ref=mixed.at[tick, b, own_rows(device)],
-            dst_ref=arrived.at[tick, owner * blocks_here + b],
-            send_sem=send_sem.at[tick, 0, b, device],
-            recv_sem=recv_sem.at[tick, 0, b, owner],
+            src_ref=mixed.at[tick, b, rows],
+            dst_ref=arrived.at[tick, owner * blocks_here + b, pl.ds(start, count)],
+            send_sem=send_sem.at[tick, 0, slot, device],
+            recv_sem=recv_sem.at[tick, 0, slot, owner],
             device_id=(section, device),
             device_id_type=MESH,
         )
 
-    def back_copy(tick, b, device, owner):
+    def back_copy(tick, b, device, owner, piece=None):
+        start, count = (0, cols) if piece is None else (piece * GROUP, GROUP)
+        slot = groups - 1 + b if piece is None else piece
+        rows = pl.ds(pl.multiple_of(owner * cols + start, count), count)
         return pltpu.make_async_remote_copy(
-            src_ref=spread.at[tick, device * blocks_here + b],
-            dst_ref=returned.at[tick, b, own_rows(owner)],
-            send_sem=send_sem.at[tick, 1, b, device],
-            recv_sem=recv_sem.at[tick, 1, b, owner],
+            src_ref=spread.at[tick, device * blocks_here + b, pl.ds(start, count)],
+            dst_ref=returned.at[tick, b, rows],
+            send_sem=send_sem.at[tick, 1, slot, device],
+            recv_sem=recv_sem.at[tick, 1, slot, owner],
             device_id=(section, device),
             device_id_type=MESH,
         )
@@ -143,12 +171,13 @@
             device_id_type=MESH,
         )
 
-    def first_factor(tick, b, source):
+    def first_factor(tick, b, source, pieces=(None,)):
         mixed[tick, b] = jnp.dot(
             right_ref[b], source[b], preferred_element_type=jnp.float32
         ).astype(jnp.bfloat16)
-        for offset in offsets:
-            out_copy(tick, b, partner(offset), here).start()
+        for piece in pieces:
+            for offset in offsets:
+                out_copy(tick, b, partner(offset), here, piece).start()
         arrived[tick, here * blocks_here + b] = mixed[tick, b, own_rows(here)]
 
     def second_factor(tick):
@@ -157,28 +186,46 @@
                 out_copy(tick, b, here, partner(offset)).wait_recv()
             return carry
 
-        lax.fori_loop(0, blocks_here, wait_block, 0)
-        piece = width // 2
-        for g in range(cols // GROUP):
+        lax.fori_loop(0, last, wait_block, 0)
+        part = width // 2
+        for g in range(groups):
+            for offset in offsets:
+                out_copy(tick, last, here, partner(offset), g).wait_recv()
             band = slice(g * GROUP, (g + 1) * GROUP)
-            for c in range(0, width, piece):
-                taken = arrived[tick, :, band, c : c + piece].reshape(-1, piece)
+            for c in range(0, width, part):
+                taken = arrived[tick, :, band, c : c + part].reshape(-1, part)
                 product = jnp.dot(expanded[g], taken, preferred_element_type=jnp.float32)
-                spread[tick, :, band, c : c + piece] = product.astype(jnp.bfloat16).reshape(
-                    -1, GROUP, piece
+                spread[tick, :, band, c : c + part] = product.astype(jnp.bfloat16).reshape(
+                    -1, GROUP, part
                 )
+            for offset in offsets:
+                back_copy(tick, 0, partner(offset), here, g).start()
 
         def send_block(b, carry):
             for offset in offsets:
                 back_copy(tick, b, partner(offset), here).start()
+            return carry
+
+        lax.fori_loop(1, blocks_here, send_block, 0)
+
+        def keep_block(b, carry):
             returned[tick, b, own_rows(here)] = spread[tick, here * blocks_here + b]
             return carry
 
-        lax.fori_loop(0, blocks_here, send_block, 0)
+        lax.fori_loop(0, blocks_here, keep_block, 0)
 
     def channel_block(tick, b, source, target):
-        for offset in offsets:
-            back_copy(tick, b, here, partner(offset)).wait_recv()
+        @pl.when(b == 0)
+        def _():
+            for g in range(groups):
+                for offset in offsets:
+                    back_copy(tick, 0, here, partner(offset), g).wait_recv()
+
+        @pl.when(b > 0)
+        def _():
+            for offset in offsets:
+                back_copy(tick, b, here, partner(offset)).wait_recv()
+
         wide = source[b].astype(jnp.float32)
         gate = jax.nn.sigmoid(wide * slope_ref[...] + shift_ref[...])
         residual = wide + returned[tick, b].astype(jnp.float32) * gate
@@ -198,12 +245,28 @@
             band = slice(k * step, (k + 1) * step)
             down = jnp.dot(hidden[k], down_ref[k], preferred_element_type=jnp.float32)
             target[b, :, band] = (residuals[:, band] + down).astype(jnp.bfloat16)
+        store(tick, b).start()
 
     def opening(b, carry):
+        load_right(b).wait()
+        load_rows(b).wait()
         first_factor(0, b, rows_ref)
         return carry
 
-    lax.fori_loop(0, blocks_here, opening, 0)
+    lax.fori_loop(0, last, opening, 0)
+    load_right(last).wait()
+    load_rows(last).wait()
+    first_factor(0, last, rows_ref, range(groups))
+
+    load_left.start()
+    load_up.start()
+    load_down.start()
+
+    @pl.when(section == 0)
+    def _():
+        load_fresh.start()
+
+    load_left.wait()
 
     total = left_ref.shape[2]
     size = total * GROUP
@@ -212,22 +275,31 @@
     same = lax.rem(lax.broadcasted_iota(jnp.int32, (size, size), 0), GROUP) == lax.rem(
         lax.broadcasted_iota(jnp.int32, (size, size), 1), GROUP
     )
-    for g in range(cols // GROUP):
-        repeated = jnp.dot(left_ref[g], repeat, preferred_element_type=jnp.float32)
+    into = lax.broadcasted_iota(jnp.int32, (size, size), 0)
+    swap = lax.rem(into, GROUP) * total + into // GROUP
+    swap = (swap == lax.broadcasted_iota(jnp.int32, (size, size), 1)).astype(jnp.bfloat16)
+    for g in range(groups):
+        swapped = jnp.dot(swap, left_ref[g], preferred_element_type=jnp.float32)
+        repeated = jnp.dot(
+            swapped.astype(jnp.bfloat16), repeat, preferred_element_type=jnp.float32
+        )
         expanded[g] = jnp.where(same, repeated, 0.0).astype(jnp.bfloat16)
+
+    load_up.wait()
+    load_down.wait()
 
     @pl.when(section == 0)
     def _():
-        relayed[...] = fresh_ref[...]
+        load_fresh.wait()
 
     second_factor(0)
 
-    def enter(b):
+    def enter(b, pieces=(None,)):
         @pl.when(section > 0)
         def _():
             relay_copy(b).wait_recv()
 
-        first_factor(1, b, relayed)
+        first_factor(1, b, relayed, pieces)
 
     def middle(b, carry):
         channel_block(0, b, rows_ref, first_ref)
@@ -243,7 +315,7 @@
         return carry
 
     lax.fori_loop(0, blocks_here, middle, 0)
-    enter(blocks_here - 1)
+    enter(last, range(groups))
     second_factor(1)
 
     def closing(b, carry):
@@ -256,15 +328,24 @@
         for offset in offsets:
             for tick in range(2):
                 out_copy(tick, b, partner(offset), here).wait_send()
-                back_copy(tick, b, partner(offset), here).wait_send()
-
-        @pl.when(section < sections - 1)
-        def _():
+                back_copy(tick, b + 1, partner(offset), here).wait_send()
+        return carry
+
+    lax.fori_loop(0, last, drain, 0)
+    for offset in offsets:
+        for tick in range(2):
+            for g in range(groups):
+                out_copy(tick, last, partner(offset), here, g).wait_send()
+                back_copy(tick, 0, partner(offset), here, g).wait_send()
+
+    @pl.when(section < sections - 1)
+    def _():
+        for b in range(blocks_here):
             relay_copy(b).wait_send()
 
-        return carry
-
-    lax.fori_loop(0, blocks_here, drain, 0)
+    for tick in range(2):
+        for b in range(blocks_here):
+            store(tick, b).wait()
 
 
 def relay_shards(
@@ -277,16 +358,24 @@
     groups = cols // GROUP
     blocked = (blocks_here, BLOCK, width)
     parts, step, wide = w_up.shape[1:]
-    left = left_factor[0].reshape(groups, GROUP, total, total).transpose(0, 2, 1, 3)
-    left = left.reshape(groups, total * GROUP, total)
+    left = left_factor.reshape(groups, GROUP * total, total)
     whole = pl.BlockSpec(memory_space=pltpu.VMEM)
+    far = pl.BlockSpec(memory_space=pl.ANY)
+    slots = blocks_here - 1 + groups
     bf16 = jnp.bfloat16
     first, second = pl.pallas_call(
         functools.partial(relay_kernel, sections, peers),
         out_shape=[jax.ShapeDtypeStruct(blocked, bf16)] * 2,
-        in_specs=[whole] * 9,
-        out_specs=[whole] * 2,
+        in_specs=[far] * 4 + [whole] * 3 + [far] * 2,
+        out_specs=[far] * 2,
         scratch_shapes=[
+            pltpu.VMEM(blocked, bf16),
+            pltpu.VMEM((blocks_here, BLOCK, BLOCK), bf16),
+            pltpu.VMEM(left.shape, bf16),
+            pltpu.VMEM((parts, step, wide), bf16),
+            pltpu.VMEM((parts, wide, step), bf16),
+            pltpu.VMEM(blocked, bf16),
+            pltpu.VMEM(blocked, bf16),
             pltpu.VMEM((2, blocks_here, BLOCK, width), bf16),
             pltpu.VMEM((2, total, cols, width), bf16),
             pltpu.VMEM((2, total, cols, width), bf16),
@@ -295,10 +384,14 @@
             pltpu.VMEM((groups, total * GROUP, total * GROUP), bf16),
             pltpu.VMEM((parts, BLOCK, wide), bf16),
             pltpu.VMEM((BLOCK, width), jnp.float32),
-            pltpu.SemaphoreType.DMA((2, 2, blocks_here, peers)),
-            pltpu.SemaphoreType.DMA((2, 2, blocks_here, peers)),
+            pltpu.SemaphoreType.DMA((2, 2, slots, peers)),
+            pltpu.SemaphoreType.DMA((2, 2, slots, peers)),
             pltpu.SemaphoreType.DMA((blocks_here,)),
             pltpu.SemaphoreType.DMA((blocks_here,)),
+            pltpu.SemaphoreType.DMA((2, blocks_here)),
+            pltpu.SemaphoreType.DMA((3,)),
+            pltpu.SemaphoreType.DMA(()),
+            pltpu.SemaphoreType.DMA((2, blocks_here)),
         ],
         compiler_params=pltpu.CompilerParams(
             collective_id=0, has_side_effects=True, vmem_limit_bytes=VMEM_LIMIT

time: 204 us -> 196 us (0.961)
  Pallas kernels: 197 us -> 191 us
    pallas_call x1, Pallas kernels: 197 us -> 191 us  [relay_shards(): pl.pallas_call(functools.partial(relay_kernel, sections, peers), out_shap...]
where the time goes in v2:
time: 196 us
  Pallas kernels  191 us (97%)
  local copies, waits for them, and re-layouts  4.55 us (2%)
    pallas_call x1, Pallas kernels, relay_shards(): pl.pallas_call(functools.partial(relay_kernel, sections, peers), out_shap...  191 us
    unnamed x4, local copies, waits for them, and re-layouts  4.55 us

profile of v2, /device:TPU:9, one launch (start us, length us, event | category | flops | bytes accessed | tf_op | source)
XLA Modules:
  0.0 196.0 jit_solution(9680913755367573605)
XLA Ops:
  0.6 190.8 %shard_map.104 = (bf16[4,256,1024]{2,1,0:T(8,128)(2,1)}, bf16[4,256,1024]{2,1,0:T(8,128)(2,1)}) custom-call(bf16[4,256,1024]{2,1,0:T(8,128)(2,1)} %bitcast.10, bf16[4,256,1024]{2,1,0:T(8,128)(2,1)} %bitcast.11, bf16[4,256,256]{2,1,0:T(8,128)(2,1)} %bitcast.14, bf16[2,512,32]{2,1,0:T(8,128)(2,1)} %bitcast.15, f32[1,1024]{1,0:T(1,128)} %slope_ref.1, ...), custom_call_target="tpu_custom_call" | custom-call | tf_op jit(solution)/shard_map/pallas_call | solution.py:366
  191.5 0.0 copy-start
  191.5 3.2 %copy.13 = bf16[1,1024,1024]{2,1,0:T(8,128)(2,1)} copy(bf16[1,1024,1024]{2,1,0:T(8,128)(2,1)} %bitcast.9) | data formatting | bytes 4194304
  194.7 0.0 copy-done
  194.7 1.3 copy.14
Async XLA Ops:
  191.5 3.2 %copy-start = (bf16[4,256,1024]{2,1,0:T(8,128)(2,1)S(1)}, bf16[4,256,1024]{2,1,0:T(8,128)(2,1)}, u32[]{:S(2)}) copy-start(bf16[4,256,1024]{2,1,0:T(8,128)(2,1)} %get-tuple-element.5) | copy-start | bytes 6291460
